TPU v7x, 128 devices: a whole 4x4x4 slice. The times are simulated.
128 devices in a mesh: leaf: 16 (over x, y), row: 4 (over z_hi, core), col: 2 (over z_lo).
Axes of the slice: x: 4, y: 4, z: 4 (z_hi: 2, z_lo: 2; z = z_hi * 2 + z_lo), core: 2. Of those that a mesh axis runs over, the one named last changes fastest.
Arguments:
- pivot_block: bfloat16 [16, 2048, 2048], P('leaf'), as said below
- coupling: float32 [16, 2048, 2048], P('leaf', ('row', 'col')), may hold values from -0.125 to 0.125, as said below
- parent_front: float32 [4, 16, 128, 8, 8, 128], P(None, 'leaf', None, None, ('row', 'col')), as said below
- child_map: int32 [16, 16], replicated, may hold values from 0 to 63, as said below
Outputs:
- pivot_factor: float32 [16, 2048, 2048], P('leaf', ('row', 'col'))
- child_below: float32 [16, 2048, 2048], P('leaf', ('row', 'col'))
- parent_factor: float32 [4, 16, 128, 8, 8, 128], P(None, 'leaf', None, None, ('row', 'col'))
Inputs may be any that keep to these rules, and one draw needn't show every extreme that they name: `pivot_block`: each pivot block is symmetric positive definite. `coupling`: Dense. `parent_front`: Symmetric; after the children's updates are subtracted the front stays positive definite. `child_map`: within a row all 16 entries differ and their residues modulo 16 run once through 0 to 15; each parent block is named by at most 4 children, and some by exactly 4.
All inputs are finite; a program needn't handle non-finite values.
Results may differ from a plain program's by a relative error of at most 0.0004.
Values sent between devices are 32-bit elements; how exact they have to be, the bound alone decides.
No kernel may reach another device: no remote copies, remote signals or barrier semaphores. Data moves between devices by JAX's collectives and lax.ppermute only.
A program may use at most 448 MiB of HBM per device.

v0:
```python
import jax
import jax.numpy as jnp
from jax import lax
from jax.sharding import PartitionSpec as P

S = 2048
NP = 8192
BLK = 128
KP = 2
PANEL = 256
UB = 16
PB = 64


HIGHEST_PREC = lax.Precision.HIGHEST


def solve_right(factor, rhs_rows):
    return lax.linalg.triangular_solve(
        factor, rhs_rows, left_side=False, lower=True, transpose_a=True
    )


def blocked_cholesky(matrix):
    order = matrix.shape[0]
    width = min(512, order)
    remain = (matrix + matrix.T) * 0.5
    columns = []
    for start in range(0, order, width):
        diag_part = jnp.linalg.cholesky(remain[:width, :width])
        lower_part = solve_right(diag_part, remain[width:, :width])
        remain = remain[width:, width:] - jnp.dot(
            lower_part, lower_part.T, precision=HIGHEST_PREC, preferred_element_type=jnp.float32
        )
        columns.append(
            jnp.concatenate([jnp.zeros((start, width), jnp.float32), diag_part, lower_part], axis=0)
        )
    return jnp.concatenate(columns, axis=1)


def class_first(block_ids, modulus, target):
    count_ids = block_ids.shape[-1]
    sort_keys = jnp.where(block_ids % modulus == target, 0, count_ids) + jnp.arange(
        count_ids, dtype=jnp.int32
    )
    return jnp.argsort(sort_keys)


def one_hot_rows(local_ids, width):
    return (local_ids[:, None] == jnp.arange(width, dtype=jnp.int32)[None, :]).astype(jnp.float32)


def local(pivot_block, coupling, parent_front, child_map):
    leaves = lax.axis_size("leaf")
    groups = lax.axis_size(("row", "col"))
    leaf_idx = lax.axis_index("leaf")
    group_idx = lax.axis_index(("row", "col"))
    row_blocks = PB // leaves
    col_blocks = PB // groups
    row_count = UB // leaves
    col_count = UB // groups
    pivot_factor = blocked_cholesky(pivot_block[0].astype(jnp.float32))
    below_own = solve_right(pivot_factor, coupling[0])
    below_all = lax.all_gather(below_own, ("row", "col"), axis=0, tiled=True)
    factor_share = S // groups
    factor_own = lax.dynamic_slice_in_dim(pivot_factor, group_idx * factor_share, factor_share, 0)
    own_map = lax.dynamic_index_in_dim(child_map, leaf_idx, 0, keepdims=False)
    below_tiles = below_all.reshape(UB, BLK, S)
    dest_order = jnp.argsort(own_map % leaves * UB + jnp.arange(UB, dtype=jnp.int32))
    send_rows = below_tiles[dest_order]
    col_order = class_first(own_map, groups, group_idx)[:col_count]
    send_cols = below_tiles[col_order].reshape(col_count * BLK, S)
    products = jnp.einsum(
        "lrs,cs->lrc",
        send_rows,
        send_cols,
        precision=HIGHEST_PREC,
        preferred_element_type=jnp.float32,
    )
    received = lax.all_to_all(products, "leaf", split_axis=0, concat_axis=0, tiled=True)

    def row_place(block_ids):
        chosen = block_ids[class_first(block_ids, leaves, leaf_idx)[:row_count]]
        return one_hot_rows(chosen // leaves, row_blocks).T

    def col_place(block_ids):
        chosen = block_ids[class_first(block_ids, groups, group_idx)[:col_count]]
        return one_hot_rows(chosen // groups, col_blocks)

    row_onehot = jax.vmap(row_place)(child_map)
    col_onehot = jax.vmap(col_place)(child_map)
    tile_grid = received.reshape(leaves, row_count, BLK, col_count, BLK)
    update = jnp.einsum(
        "cjq,cqakb,ckl->jalb",
        row_onehot,
        tile_grid,
        col_onehot,
        precision=HIGHEST_PREC,
        preferred_element_type=jnp.float32,
    )
    local_rows = row_blocks * BLK
    local_cols = col_blocks * BLK
    front_local = parent_front.reshape(local_rows, local_cols) - update.reshape(
        local_rows, local_cols
    )
    block_iota = jnp.arange(BLK, dtype=jnp.int32)[None, :]
    row_global = (
        (jnp.arange(row_blocks, dtype=jnp.int32)[:, None] * leaves + leaf_idx) * BLK + block_iota
    ).reshape(-1)
    col_global = (
        (jnp.arange(col_blocks, dtype=jnp.int32)[:, None] * groups + group_idx) * BLK + block_iota
    ).reshape(-1)
    for panel_idx in range(KP):
        first_col = panel_idx * PANEL
        after_col = first_col + PANEL
        block_low = first_col // BLK
        block_high = block_low + 1
        by_blocks = front_local.reshape(local_rows, col_blocks, BLK)
        part_low = jnp.where(
            group_idx == block_low % groups, by_blocks[:, block_low // groups], 0.0
        )
        part_high = jnp.where(
            group_idx == block_high % groups, by_blocks[:, block_high // groups], 0.0
        )
        own_panel = lax.psum(jnp.concatenate([part_low, part_high], axis=1), ("row", "col"))
        panel_tiles = own_panel.reshape(row_blocks, BLK, PANEL)
        diag_low = jnp.where(leaf_idx == block_low % leaves, panel_tiles[block_low // leaves], 0.0)
        diag_high = jnp.where(
            leaf_idx == block_high % leaves, panel_tiles[block_high // leaves], 0.0
        )
        diag_low, diag_high = lax.psum((diag_low, diag_high), "leaf")
        diag_factor = jnp.linalg.cholesky(jnp.concatenate([diag_low, diag_high], axis=0))
        solved_own = solve_right(diag_factor, own_panel)
        in_panel = (row_global >= first_col) & (row_global < after_col)
        from_diag = diag_factor[jnp.clip(row_global - first_col, 0, PANEL - 1)]
        row_part = jnp.where((row_global >= after_col)[:, None], solved_own, 0.0)
        row_part = jnp.where(in_panel[:, None], from_diag, row_part)
        gathered = lax.all_gather(
            row_part.reshape(row_blocks, 1, BLK, PANEL), "leaf", axis=1, tiled=True
        ).reshape(NP, PANEL)
        col_part = lax.dynamic_index_in_dim(
            gathered.reshape(col_blocks, groups, BLK, PANEL), group_idx, 1, keepdims=False
        ).reshape(local_cols, PANEL)
        row_trail = jnp.where((row_global >= after_col)[:, None], row_part, 0.0)
        col_trail = jnp.where((col_global >= after_col)[:, None], col_part, 0.0)
        front_local = front_local - jnp.dot(
            row_trail, col_trail.T, precision=HIGHEST_PREC, preferred_element_type=jnp.float32
        )
        picked = jnp.take(row_part, jnp.clip(col_global - first_col, 0, PANEL - 1), axis=1)
        in_cols = (col_global >= first_col) & (col_global < after_col)
        front_local = jnp.where(in_cols[None, :], picked, front_local)
        in_rows = (row_global >= first_col) & (row_global < after_col)
        front_local = jnp.where(
            in_rows[:, None] & (col_global >= after_col)[None, :], 0.0, front_local
        )
    return (
        factor_own[None],
        below_own[None],
        front_local.reshape(row_blocks, 1, BLK, col_blocks, 1, BLK),
    )


def solution(mesh):
    return jax.shard_map(
        local,
        mesh=mesh,
        in_specs=(
            P("leaf", None, None),
            P("leaf", ("row", "col"), None),
            P(None, "leaf", None, None, ("row", "col"), None),
            P(),
        ),
        out_specs=(
            P("leaf", ("row", "col"), None),
            P("leaf", ("row", "col"), None),
            P(None, "leaf", None, None, ("row", "col"), None),
        ),
        check_vma=False,
    )
```

profile of v0, /device:TPU:0, one launch (start us, length us, event | category | flops | bytes accessed | tf_op | source)
XLA Modules:
  0.0 1930.3 jit_solution(368382341850936591)
XLA Ops:
  7.2 11.2 bitcast_convert_fusion
  18.4 17.6 copy.46
  36.0 14.6 fusion
  53.8 11.7 cholesky.541
  76.1 11.7 cholesky.560
  98.5 11.7 cholesky.581
  120.7 11.7 cholesky.594
  146.9 39.3 %custom-call.38 = f32[4,128,128]{1,2,0:T(8,128)S(1)} custom-call(f32[4,128,128]{2,1,0:T(8,128)S(1)} %get-tuple-element.31), custom_call_target="InvertDiagBlocksLowerTriangular" | custom-call | tf_op jit(solution)/shard_map/triangular_solve | solution.py:19
  202.5 19.4 %slice_subtract_fusion = f32[1536,1536]{0,1:T(8,128)S(1)} fusion(f32[2048,2048]{0,1:T(8,128)} %fusion, f32[1536,128]{1,0:T(8,128)S(1)} %fusion.191, f32[1536,128]{1,0:T(8,128)S(1)} %copy.50, f32[1536,128]{1,0:T(8,128)S(1)} %copy.49, f32[1536,128]{1,0:T(8,128)S(1)} %copy.48), kind=kOutput, calls=%fused_computation.26 | convolution fusion | flops 14500233216 | bytes 22020096 | tf_op jit(solution)/shard_map/dot_general | solution.py:32
  230.6 11.7 cholesky.609
  254.8 11.7 cholesky.628
  266.6 10.0 custom-call.68
  278.1 11.7 cholesky.649
  301.1 11.7 cholesky.662
  320.1 11.8 while.9
  331.9 39.3 %custom-call.39 = f32[4,128,128]{1,2,0:T(8,128)S(1)} custom-call(f32[4,128,128]{2,1,0:T(8,128)S(1)} %get-tuple-element.39), custom_call_target="InvertDiagBlocksLowerTriangular" | custom-call | tf_op jit(solution)/shard_map/triangular_solve | solution.py:19
  403.6 11.7 cholesky.677
  427.8 11.7 cholesky.696
  439.6 10.2 custom-call.71
  451.3 11.7 cholesky.717
  474.3 11.7 cholesky.730
  493.0 11.4 while.10
  504.4 39.3 %custom-call.40 = f32[4,128,128]{1,2,0:T(8,128)S(1)} custom-call(f32[4,128,128]{2,1,0:T(8,128)S(1)} %get-tuple-element.47), custom_call_target="InvertDiagBlocksLowerTriangular" | custom-call | tf_op jit(solution)/shard_map/triangular_solve | solution.py:19
  561.8 11.7 cholesky.745
  587.3 11.7 cholesky.764
  613.1 13.2 cholesky.785
  627.7 11.4 custom-call.75
  641.4 11.7 cholesky.798
  660.8 41.0 %fusion.1 = (f32[2048,2048]{1,0:T(8,128)}, f32[2048,2048]{1,0:T(8,128)}) fusion(f32[512,512]{1,0:T(8,128)S(1)} %select_select_fusion, f32[512,128]{1,0:T(8,128)} %copy-done.23, f32[512,128]{1,0:T(8,128)S(1)} %copy.62, f32[512,128]{1,0:T(8,128)} %copy.61, f32[512,128]{1,0:T(8,128)} %copy.60, f32[512,512]{1,0:T(8,128)} %get-tuple-element.131, ...), kind=kLoop, calls=%fused_computation.25 | loop fusion | flops 88080384 | bytes 47185920 | tf_op jit(solution)/shard_map/triangular_solve | solution.py:19
  701.8 56.1 %while.11 = (s32[]{:T(128)}, f32[2048,2048]{1,0:T(8,128)}, s32[16,2]{0,1:T(2,128)S(1)}, f32[16,128,128]{2,1,0:T(8,128)}, s32[]{:T(128)}) while((s32[]{:T(128)}, f32[2048,2048]{1,0:T(8,128)}, s32[16,2]{0,1:T(2,128)S(1)}, f32[16,128,128]{2,1,0:T(8,128)}, s32[]{:T(128)}) %tuple.280), condition=%wide.while_cond.4, body=%wide.while_body.4.sunk | while | flops 2 | bytes 132205 | solution.py:19
  757.9 158.2 %custom-call.41 = f32[16,128,128]{1,2,0:T(8,128)S(1)} custom-call(f32[16,128,128]{2,1,0:T(8,128)} %get-tuple-element.55), custom_call_target="InvertDiagBlocksLowerTriangular" | custom-call | tf_op jit(solution)/shard_map/triangular_solve | solution.py:19
  971.0 247.0 %all-gather.4.cloned.1.call-done = f32[2048,2048]{0,1:T(8,128)} async-done(((f32[256,2048]{0,1:T(8,128)}), f32[2048,2048]{0,1:T(8,128)}) %all-gather.4.cloned.1.call-update) | async-done | bytes 16777232 | tf_op jit(solution)/shard_map/all_gather | solution.py:64
  1218.0 17.6 copy.112
  1235.6 13.8 gather_fusion
  1255.9 17.0 fusion.283
  1285.1 22.4 %all-to-all-done = f32[16,128,256]{2,1,0:T(8,128)S(1)} async-done(((f32[16,128,256]{2,1,0:T(8,128)}), f32[16,128,256]{2,1,0:T(8,128)S(1)}, u32[]{:S(2)}, u32[]{:S(2)}) %all-to-all-start) | async-done | bytes 2097184 | tf_op jit(solution)/shard_map/all_to_all | solution.py:80
  1330.6 59.1 %all-reduce.10.cloned.1.call-done = f32[512,256]{0,1:T(8,128)} async-done(((f32[512,256]{0,1:T(8,128)}), f32[512,256]{0,1:T(8,128)}) %all-reduce.10.cloned.1.call-update) | async-done | bytes 524304 | tf_op jit(solution)/shard_map/psum | solution.py:125
  1391.8 85.0 %all-reduce.16.cloned.1.call-done = (f32[128,256]{0,1:T(8,128)}, f32[128,256]{0,1:T(8,128)}) async-done(((f32[128,256]{0,1:T(8,128)}, f32[128,256]{0,1:T(8,128)}), (f32[128,256]{0,1:T(8,128)}, f32[128,256]{0,1:T(8,128)})) %all-reduce.16.cloned.1.call-update) | async-done | bytes 262160 | tf_op jit(solution)/shard_map/psum | solution.py:131
  1478.9 11.7 cholesky.813
  1501.0 11.7 cholesky.823
  1522.0 19.7 %custom-call.77 = f32[2,128,128]{1,2,0:T(8,128)S(1)} custom-call(f32[2,128,128]{2,1,0:T(8,128)S(1)} %get-tuple-element.62), custom_call_target="InvertDiagBlocksLowerTriangular" | custom-call | tf_op jit(solution)/shard_map/triangular_solve/custom-call.13 | solution.py:19
  1554.2 62.1 %all-gather.6.cloned.1.call-done = f32[4,16,128,256]{3,2,1,0:T(8,128)} async-done(((f32[4,1,128,256]{3,2,1,0:T(8,128)}), f32[4,16,128,256]{3,2,1,0:T(8,128)}) %all-gather.6.cloned.1.call-update) | async-done | bytes 8388624 | tf_op jit(solution)/shard_map/all_gather | solution.py:138
  1628.5 60.7 %all-reduce.12.cloned.1.call-done = f32[512,256]{0,1:T(8,128)} async-done(((f32[512,256]{0,1:T(8,128)}), f32[512,256]{0,1:T(8,128)}) %all-reduce.12.cloned.1.call-update) | async-done | bytes 524304 | tf_op jit(solution)/shard_map/psum | solution.py:125
  1691.1 85.2 %all-reduce.14.cloned.1.call-done = (f32[128,256]{0,1:T(8,128)}, f32[128,256]{0,1:T(8,128)}) async-done(((f32[128,256]{0,1:T(8,128)}, f32[128,256]{0,1:T(8,128)}), (f32[128,256]{0,1:T(8,128)}, f32[128,256]{0,1:T(8,128)})) %all-reduce.14.cloned.1.call-update) | async-done | bytes 262160 | tf_op jit(solution)/shard_map/psum | solution.py:131
  1778.3 11.7 cholesky.840
  1800.4 11.7 cholesky.850
  1821.4 19.7 %custom-call.79 = f32[2,128,128]{1,2,0:T(8,128)S(1)} custom-call(f32[2,128,128]{2,1,0:T(8,128)S(1)} %get-tuple-element.63), custom_call_target="InvertDiagBlocksLowerTriangular" | custom-call | tf_op jit(solution)/shard_map/triangular_solve/custom-call.13 | solution.py:19
  1859.3 56.4 %all-gather.8.cloned.1.call-done = f32[4,16,128,256]{3,2,1,0:T(8,128)} async-done(((f32[4,1,128,256]{3,2,1,0:T(8,128)}), f32[4,16,128,256]{3,2,1,0:T(8,128)}) %all-gather.8.cloned.1.call-update) | async-done | bytes 8388624 | tf_op jit(solution)/shard_map/all_gather | solution.py:138
  (458 shorter events, 503.7 us)
Async XLA Ops:
  7.2 1210.9 %all-gather.4.cloned.1.call-start = ((), (), s32[]{:S(2)}) async-start(), calls=%async_computation.1 | async-start | bytes 18874368 | tf_op jit(solution)/shard_map/all_gather | solution.py:64
  146.9 44.3 %copy-start.19 = (f32[512,512]{1,0:T(8,128)}, f32[512,512]{1,0:T(8,128)S(1)}, u32[]{:S(2)}) copy-start(f32[512,512]{1,0:T(8,128)S(1)} %get-tuple-element.647) | copy-start | bytes 3145732
  186.3 4.1 copy-start.28
  199.7 22.2 %copy-start.7 = (f32[1536,128]{1,0:T(8,128)}, f32[1536,128]{1,0:T(8,128)S(1)}, u32[]{:S(2)}) copy-start(f32[1536,128]{1,0:T(8,128)S(1)} %copy.48) | copy-start | bytes 2359300
  202.5 19.4 %copy-start.9 = (f32[1536,128]{1,0:T(8,128)}, f32[1536,128]{1,0:T(8,128)S(1)}, u32[]{:S(2)}) copy-start(f32[1536,128]{1,0:T(8,128)S(1)} %fusion.191) | copy-start | bytes 2359300
  221.9 3.6 copy-start.1
  229.6 1.0 copy-start.21
  377.6 0.8 copy-start.16
  383.8 3.0 copy-start.11
  386.9 9.7 copy-start.14
  396.6 1.9 copy-start.2
  402.6 1.0 copy-start.22
  543.8 5.2 copy-start.29
  553.9 0.7 copy-start.23
  560.8 1.0 copy-start.20
  586.5 0.8 copy-start.27
  658.3 1.2 copy-start.17
  658.3 1.5 copy-start.18
  658.5 1.6 copy-start.8
  658.5 1.9 copy-start.10
  658.5 2.0 copy-start.12
  658.5 2.2 copy-start.13
  658.5 2.3 copy-start.15
  916.1 3.3 copy-start.26
  962.2 6.2 copy-start
  967.0 1.3 copy-start.3
  1273.0 34.6 %all-to-all-start = ((f32[16,128,256]{2,1,0:T(8,128)}), f32[16,128,256]{2,1,0:T(8,128)S(1)}, u32[]{:S(2)}, u32[]{:S(2)}) async-start(f32[16,128,256]{2,1,0:T(8,128)} %fusion.283), calls=%async_computation | async-start | bytes 4194304 | tf_op jit(solution)/shard_map/all_to_all | solution.py:80
  1279.8 109.9 %all-reduce.10.cloned.1.call-start = ((), (), s32[]{:S(2)}) async-start(), calls=%async_computation.2 | async-start | bytes 1048576 | tf_op jit(solution)/shard_map/psum | solution.py:125
  1330.4 146.5 %all-reduce.16.cloned.1.call-start = ((), (), s32[]{:S(2)}) async-start(), calls=%async_computation.7 | async-start | bytes 524288 | tf_op jit(solution)/shard_map/psum | solution.py:131
  1391.3 225.0 %all-gather.6.cloned.1.call-start = ((), (), s32[]{:S(2)}) async-start(), calls=%async_computation.3 | async-start | bytes 8912896 | tf_op jit(solution)/shard_map/all_gather | solution.py:138
  1518.1 26.8 %copy-start.25 = (f32[512,256]{0,1:T(8,128)S(1)}, f32[512,256]{0,1:T(8,128)}, u32[]{:S(2)}) copy-start(f32[512,256]{0,1:T(8,128)} %copy.84) | copy-start | bytes 1572868
  1546.1 143.1 %all-reduce.12.cloned.1.call-start = ((), (), s32[]{:S(2)}) async-start(), calls=%async_computation.4 | async-start | bytes 1048576 | tf_op jit(solution)/shard_map/psum | solution.py:125
  1616.3 1.9 copy-start.5
  1616.3 2.5 copy-start.6
  1628.4 147.9 %all-reduce.14.cloned.1.call-start = ((), (), s32[]{:S(2)}) async-start(), calls=%async_computation.6 | async-start | bytes 524288 | tf_op jit(solution)/shard_map/psum | solution.py:131
  1690.8 224.9 %all-gather.8.cloned.1.call-start = ((), (), s32[]{:S(2)}) async-start(), calls=%async_computation.5 | async-start | bytes 8912896 | tf_op jit(solution)/shard_map/all_gather | solution.py:138
  1817.6 26.7 %copy-start.24 = (f32[512,256]{0,1:T(8,128)S(1)}, f32[512,256]{0,1:T(8,128)}, u32[]{:S(2)}) copy-start(f32[512,256]{0,1:T(8,128)} %copy.91) | copy-start | bytes 1572868
  1915.7 1.9 copy-start.4
Sparse Core Ops, SparseCore 0:
  968.5 249.5 all-gather.3
  1330.6 59.0 all-reduce.9
  1393.8 83.0 all-reduce.15
  1546.2 70.0 all-gather.5
  1628.5 60.6 all-reduce.11
  1693.1 83.1 all-reduce.13
  1845.6 70.0 all-gather.7
where the time goes:
time: 1940 us; the launch traced here: 1930 us
  other arithmetic  795 us (41%)
  waiting for transfers between devices  678 us (35%)
  local copies, waits for them, and re-layouts  234 us (12%)
  matrix products  186 us (10%)
  between operations  29.5 us (2%)
    another operation x15, other arithmetic, solve_right(): lax.linalg.triangular_solve(factor, rhs_rows, left_side=False, lower=True...  361 us
    another operation x59, other arithmetic, blocked_cholesky(): diag_part = jnp.linalg.cholesky(remain[:width, :width])  321 us
    all_gather x1, waiting for transfers between devices, local(): below_all = lax.all_gather(below_own, ('row', 'col'), axis=0, tiled=True)  247 us
    psum x2, waiting for transfers between devices, local(): diag_low, diag_high = lax.psum((diag_low, diag_high), 'leaf')  170 us
    psum x2, waiting for transfers between devices, local(): lax.psum(jnp.concatenate([part_low, part_high], axis=1), ('row', 'col'))  120 us
    all_gather x2, waiting for transfers between devices, local(): lax.all_gather(row_part.reshape(row_blocks, 1, BLK, PANEL), 'leaf', axis=...  118 us
    another operation x58, matrix products, solve_right(): lax.linalg.triangular_solve(factor, rhs_rows, left_side=False, lower=True...  92.1 us
    another operation x85, local copies, waits for them, and re-layouts  89.8 us
  transfers between devices with their start and end apart: 8, of which 8 were waited for; matrix products, arithmetic and copies ran while one was open for 2% of the time, Pallas kernels for 0%

commit v1 on v0

v1 whole, which is shorter than its diff:
```python
import functools

import jax
import jax.numpy as jnp
from jax import lax
from jax.experimental import pallas as pl
from jax.experimental.pallas import tpu as pltpu
from jax.sharding import PartitionSpec as P

F32 = jnp.float32
BF16 = jnp.bfloat16
S = 2048
BLK = 128
PIVOTS = 512
LEAVES = 16
GROUPS = 8
NB = 256
HB = 128
SUB = 8
STEPS = S // NB
VMEM = pltpu.VMEM
SMEM = pltpu.SMEM
GROUP = ("row", "col")


def dot_t(a, b):
    return lax.dot_general(a, b, (((1,), (1,)), ((), ())), preferred_element_type=F32)


def dot_n(a, b):
    return lax.dot_general(a, b, (((1,), (0,)), ((), ())), preferred_element_type=F32)


def halves(x):
    high = x.astype(BF16)
    low = (x - high.astype(F32)).astype(BF16)
    return high, low


def left3(x, axis=1):
    high, low = halves(x)
    return jnp.concatenate([high, high, low], axis=axis)


def right3(x, axis=1):
    high, low = halves(x)
    return jnp.concatenate([high, low, high], axis=axis)


def mul_t(a, b):
    return dot_t(left3(a), right3(b))


def mul_n(a, b):
    return dot_n(left3(a), right3(b, axis=0))


def eliminate(rows, base):
    sub = lax.broadcasted_iota(jnp.int32, (SUB, HB), 0)
    sub_wide = lax.broadcasted_iota(jnp.int32, rows.shape, 0)
    cols = [jnp.broadcast_to(rows[:, base + j : base + j + 1], (SUB, HB)) for j in range(SUB)]
    for k in range(SUB):
        inv = lax.rsqrt(jnp.broadcast_to(cols[k][k : k + 1, :], (SUB, HB)))
        scaled = cols[k] * inv
        below = jnp.where(sub > k, scaled, 0.0)
        for j in range(k + 1, SUB):
            cols[j] = cols[j] - below * jnp.broadcast_to(scaled[j : j + 1, :], (SUB, HB))
        pivot_row = jnp.broadcast_to(rows[k : k + 1, :], rows.shape) * jnp.concatenate(
            [inv, inv], axis=1
        )
        below_wide = jnp.concatenate([below, below], axis=1)
        rows = jnp.where(sub_wide == k, pivot_row, rows - below_wide * pivot_row)
    return rows


def diag_small(block, work):
    row = lax.broadcasted_iota(jnp.int32, (HB, HB), 0)
    col = lax.broadcasted_iota(jnp.int32, (HB, HB), 1)
    work[:, :HB] = block
    work[:, HB:] = jnp.where(row == col, 1.0, 0.0)
    for base in range(0, HB, SUB):
        rows = eliminate(work[base : base + SUB, :], base)
        work[base : base + SUB, :] = rows
        after = base + SUB
        if after < HB:
            high = rows.astype(BF16).astype(F32)
            low = rows - high
            left = jnp.concatenate([high[:, :HB], high[:, :HB], low[:, :HB]], axis=0).astype(BF16)
            right = jnp.concatenate([high, low, high], axis=0).astype(BF16)
            product = lax.dot_general(
                left, right, (((0,), (0,)), ((), ())), preferred_element_type=F32
            )
            work[after:, :] = work[after:, :] - product[after:, :]
    return jnp.where(col >= row, work[:, :HB], 0.0), work[:, HB:]


def diag_block(block, work):
    upper_a, inv_a = diag_small(block[:HB, :HB], work)
    low_left = mul_t(block[HB:, :HB], inv_a)
    upper_b, inv_b = diag_small(block[HB:, HB:] - mul_t(low_left, low_left), work)
    inv_low = -mul_n(inv_b, mul_n(low_left, inv_a))
    zero = jnp.zeros((HB, HB), F32)
    factor = jnp.concatenate(
        [
            jnp.concatenate([upper_a.T, zero], axis=1),
            jnp.concatenate([low_left, upper_b.T], axis=1),
        ],
        axis=0,
    )
    inverse = jnp.concatenate(
        [
            jnp.concatenate([inv_a, zero], axis=1),
            jnp.concatenate([inv_low, inv_b], axis=1),
        ],
        axis=0,
    )
    return factor, inverse


def part(i):
    return pl.ds(pl.multiple_of(i * NB, NB), NB)


def factor_kernel(p_ref, c_ref, l_ref, b_ref, inv_ref, work, left, right):
    def load_row(i, _):
        def load(k, _):
            l_ref[part(i), part(k)] = p_ref[part(i), part(k)].astype(F32)
            return 0

        def clear(k, _):
            l_ref[part(i), part(k)] = jnp.zeros((NB, NB), F32)
            return 0

        lax.fori_loop(0, i + 1, load, 0)
        lax.fori_loop(i + 1, STEPS, clear, 0)
        return 0

    lax.fori_loop(0, STEPS, load_row, 0)
    b_ref[...] = c_ref[...]

    def step(j, _):
        factor, inverse = diag_block(l_ref[part(j), part(j)], work)
        l_ref[part(j), part(j)] = factor
        inv_ref[j] = inverse
        inverse_parts = right3(inverse)
        own = dot_t(left3(b_ref[:, part(j)]), inverse_parts)
        b_ref[:, part(j)] = own
        own_parts = left3(own)

        def panel(i, _):
            x = dot_t(left3(l_ref[part(i), part(j)]), inverse_parts)
            l_ref[part(i), part(j)] = x
            left[part(i), :] = left3(x)
            right[part(i), :] = right3(x)
            return 0

        lax.fori_loop(j + 1, STEPS, panel, 0)

        def trail(k, _):
            b_ref[:, part(k)] = b_ref[:, part(k)] - dot_t(own_parts, right[part(k), :])

            def trail_row(i, _):
                l_ref[part(i), part(k)] = l_ref[part(i), part(k)] - dot_t(
                    left[part(i), :], right[part(k), :]
                )
                return 0

            lax.fori_loop(k, STEPS, trail_row, 0)
            return 0

        lax.fori_loop(j + 1, STEPS, trail, 0)
        return 0

    lax.fori_loop(0, STEPS, step, 0)


def factor_child(pivot, coupling):
    return pl.pallas_call(
        factor_kernel,
        out_shape=(
            jax.ShapeDtypeStruct((S, S), F32),
            jax.ShapeDtypeStruct((NB, S), F32),
            jax.ShapeDtypeStruct((STEPS, NB, NB), F32),
        ),
        in_specs=[pl.BlockSpec(memory_space=VMEM)] * 2,
        out_specs=(pl.BlockSpec(memory_space=VMEM),) * 3,
        scratch_shapes=[
            VMEM((HB, 2 * HB), F32),
            VMEM((S, 3 * NB), BF16),
            VMEM((S, 3 * NB), BF16),
        ],
        compiler_params=pltpu.CompilerParams(vmem_limit_bytes=56 * 2**20),
        cost_estimate=pl.CostEstimate(
            flops=150 * 10**9, bytes_accessed=30 * 2**20, transcendentals=0
        ),
    )(pivot, coupling)


SOLVED = 3


def solve_kernel(l_hbm, inv_ref, *refs):
    ins = refs[:SOLVED]
    outs = refs[SOLVED : 2 * SOLVED]
    l_vmem, c_vmem, high, low, sems = refs[2 * SOLVED :]

    def l_copy(j):
        where = (pl.ds(j * NB, NB), pl.ds(0, (j + 1) * NB))
        return pltpu.make_async_copy(l_hbm.at[where], l_vmem.at[where], sems.at[j])

    def c_copy(j, i):
        cols = pl.ds(j * NB, NB)
        return pltpu.make_async_copy(
            ins[i].at[:, cols], c_vmem.at[pl.ds(i * NB, NB), cols], sems.at[STEPS + j * SOLVED + i]
        )

    for j in range(STEPS):
        l_copy(j).start()
        for i in range(SOLVED):
            c_copy(j, i).start()
    for j in range(STEPS):
        l_copy(j).wait()
        for i in range(SOLVED):
            c_copy(j, i).wait()
        rhs = c_vmem[:, j * NB : (j + 1) * NB]
        if j:
            before = slice(0, j * NB)
            f_high, f_low = halves(l_vmem[j * NB : (j + 1) * NB, before])
            rhs = rhs - (
                dot_t(high[:, before], f_high)
                + dot_t(high[:, before], f_low)
                + dot_t(low[:, before], f_high)
            )
        x = mul_t(rhs, inv_ref[j])
        x_high, x_low = halves(x)
        high[:, j * NB : (j + 1) * NB] = x_high
        low[:, j * NB : (j + 1) * NB] = x_low
        for i in range(SOLVED):
            outs[i][:, j * NB : (j + 1) * NB] = x[i * NB : (i + 1) * NB]


def solve_rows(factor, inverses, rows):
    return pl.pallas_call(
        solve_kernel,
        out_shape=(jax.ShapeDtypeStruct((NB, S), F32),) * SOLVED,
        in_specs=[pl.BlockSpec(memory_space=pl.ANY), pl.BlockSpec(memory_space=VMEM)]
        + [pl.BlockSpec(memory_space=pl.ANY)] * SOLVED,
        out_specs=(pl.BlockSpec(memory_space=VMEM),) * SOLVED,
        scratch_shapes=[
            VMEM((S, S), F32),
            VMEM((SOLVED * NB, S), F32),
            VMEM((SOLVED * NB, S), BF16),
            VMEM((SOLVED * NB, S), BF16),
            pltpu.SemaphoreType.DMA((STEPS * (1 + SOLVED),)),
        ],
        compiler_params=pltpu.CompilerParams(vmem_limit_bytes=56 * 2**20),
        cost_estimate=pl.CostEstimate(
            flops=20 * 10**9, bytes_accessed=24 * 2**20, transcendentals=0
        ),
    )(factor, inverses, *rows)


def update_kernel(place, map_ref, *refs):
    ins = refs[:GROUPS]
    out, tiles, chosen, high, low, sems = refs[GROUPS:]
    leaf = place[0]
    group = place[1]
    for s in range(GROUPS):
        for half in range(2):
            tile = (group ^ s) * 2 + half
            dest = lax.rem(map_ref[leaf, tile], LEAVES)
            rows = pl.ds(half * BLK, BLK)
            pltpu.make_async_copy(ins[s].at[rows, :], tiles.at[dest], sems.at[dest]).start()
            for pick in range(2):

                @pl.when(dest == group + pick * GROUPS)
                def _():
                    pltpu.make_async_copy(
                        ins[s].at[rows, :],
                        chosen.at[pl.ds(pick * BLK, BLK), :],
                        sems.at[LEAVES + pick],
                    ).start()

    for pick in range(2):
        pltpu.make_async_copy(
            ins[0].at[pl.ds(0, BLK), :],
            chosen.at[pl.ds(pick * BLK, BLK), :],
            sems.at[LEAVES + pick],
        ).wait()
    high[...], low[...] = halves(chosen[...])
    together = 4

    def tile_group(q, _):
        for t in range(together):
            pltpu.make_async_copy(
                ins[0].at[pl.ds(0, BLK), :],
                tiles.at[q * together + t],
                sems.at[q * together + t],
            ).wait()
        rows = tiles[pl.ds(q * together, together)].reshape(together * BLK, S)
        r_high, r_low = halves(rows)
        product = (
            dot_t(r_high, high[...]) + dot_t(r_high, low[...]) + dot_t(r_low, high[...])
        )
        for t in range(together):
            for pick in range(2):
                out[q * together + t, pick] = product[
                    t * BLK : (t + 1) * BLK, pick * BLK : (pick + 1) * BLK
                ]
        return 0

    lax.fori_loop(0, LEAVES // together, tile_group, 0)


def update_blocks(place, child_map, rows):
    return pl.pallas_call(
        update_kernel,
        out_shape=jax.ShapeDtypeStruct((LEAVES, 2, BLK, BLK), F32),
        in_specs=[pl.BlockSpec(memory_space=SMEM)] * 2
        + [pl.BlockSpec(memory_space=pl.ANY)] * GROUPS,
        out_specs=pl.BlockSpec(memory_space=VMEM),
        scratch_shapes=[
            VMEM((LEAVES, BLK, S), F32),
            VMEM((2 * BLK, S), F32),
            VMEM((2 * BLK, S), BF16),
            VMEM((2 * BLK, S), BF16),
            pltpu.SemaphoreType.DMA((LEAVES + 2,)),
        ],
        compiler_params=pltpu.CompilerParams(vmem_limit_bytes=56 * 2**20),
        cost_estimate=pl.CostEstimate(
            flops=8 * 10**9, bytes_accessed=20 * 2**20, transcendentals=0
        ),
    )(place, child_map, *rows)


def assemble_kernel(place, map_ref, got, parent, front, row_level, col_slot):
    leaf = place[0]
    group = place[1]

    def find(c, _):
        level = jnp.int32(0)
        slots = [jnp.int32(0), jnp.int32(0)]
        for t in range(LEAVES):
            block = map_ref[c, t]
            residue = block & (LEAVES - 1)
            level = jnp.where(residue == leaf, block >> 4, level)
            for pick in range(2):
                slots[pick] = jnp.where(
                    residue == group + pick * GROUPS, block >> 3, slots[pick]
                )
        row_level[c] = level
        for pick in range(2):
            col_slot[c, pick] = slots[pick]
        return 0

    lax.fori_loop(0, LEAVES, find, 0)
    for k in range(8):
        front[k] = parent[pl.ds(k, 4 * BLK, 8), :]

    def subtract(c, _):
        rows = pl.ds(pl.multiple_of(row_level[c] * BLK, BLK), BLK)
        for pick in range(2):
            slot = col_slot[c, pick]
            front[slot, rows, :] = front[slot, rows, :] - got[c, pick]
        return 0

    lax.fori_loop(0, LEAVES, subtract, 0)


def assemble(place, child_map, got, parent):
    return pl.pallas_call(
        assemble_kernel,
        out_shape=jax.ShapeDtypeStruct((8, 4 * BLK, BLK), F32),
        in_specs=[pl.BlockSpec(memory_space=SMEM)] * 2 + [pl.BlockSpec(memory_space=VMEM)] * 2,
        out_specs=pl.BlockSpec(memory_space=VMEM),
        scratch_shapes=[SMEM((LEAVES,), jnp.int32), SMEM((LEAVES, 2), jnp.int32)],
        compiler_params=pltpu.CompilerParams(vmem_limit_bytes=32 * 2**20),
        cost_estimate=pl.CostEstimate(
            flops=10**6, bytes_accessed=6 * 2**20, transcendentals=0
        ),
    )(place, child_map, got, parent)


def panel_kernel(place, d0, d1, d2, d3, l_ref, inv_ref, block, work):
    group = place[1]
    for i, ref in enumerate((d0, d1, d2, d3)):
        block[(group & 3) ^ i] = ref[...]

    def square(r, c):
        rows = slice(r * NB, (r + 1) * NB)
        return jnp.concatenate([block[2 * c, rows, :], block[2 * c + 1, rows, :]], axis=1)

    factor_a, inv_a = diag_block(square(0, 0), work)
    low_left = mul_t(square(1, 0), inv_a)
    factor_b, inv_b = diag_block(square(1, 1) - mul_t(low_left, low_left), work)
    zero = jnp.zeros((NB, NB), F32)
    l_ref[:NB, :NB] = factor_a
    l_ref[:NB, NB:] = zero
    l_ref[NB:, :NB] = low_left
    l_ref[NB:, NB:] = factor_b
    inv_ref[:NB, :NB] = inv_a
    inv_ref[:NB, NB:] = zero
    inv_ref[NB:, :NB] = -mul_n(inv_b, mul_n(low_left, inv_a))
    inv_ref[NB:, NB:] = inv_b


def factor_panel(place, columns):
    return pl.pallas_call(
        panel_kernel,
        out_shape=(jax.ShapeDtypeStruct((PIVOTS, PIVOTS), F32),) * 2,
        in_specs=[pl.BlockSpec(memory_space=SMEM)] + [pl.BlockSpec(memory_space=VMEM)] * 4,
        out_specs=(pl.BlockSpec(memory_space=VMEM),) * 2,
        scratch_shapes=[VMEM((4, PIVOTS, BLK), F32), VMEM((HB, 2 * HB), F32)],
        compiler_params=pltpu.CompilerParams(vmem_limit_bytes=32 * 2**20),
        cost_estimate=pl.CostEstimate(
            flops=25 * 10**9, bytes_accessed=4 * 2**20, transcendentals=0
        ),
    )(place, *columns)


def trailing_kernel(
    place, front, x0, x1, x2, x3, y0, y1, y2, y3, l_ref, inv_ref, out, panel, above
):
    leaf = place[0]
    group = place[1]
    for i, ref in enumerate((x0, x1, x2, x3)):
        panel[(group & 3) ^ i] = ref[...]
    for i, ref in enumerate((y0, y1, y2, y3)):
        above[(leaf - i) & 3] = ref[...]
    inverse = inv_ref[...]
    own = jnp.concatenate([panel[i] for i in range(4)], axis=1)
    solved = mul_t(own, inverse)
    solved_parts = left3(solved)
    inverse_parts = left3(inverse)
    row = lax.broadcasted_iota(jnp.int32, (PIVOTS, BLK), 0)
    in_panel = (row < BLK) & (leaf < 4)
    for pair in range(4):
        across = jnp.concatenate(
            [
                jnp.concatenate([above[q, 2 * pair], above[q, 2 * pair + 1]], axis=1)
                for q in range(4)
            ],
            axis=0,
        )
        across = dot_n(inverse_parts, right3(across, axis=0))
        change = dot_n(solved_parts, right3(across, axis=0))
        for half in range(2):
            k = 2 * pair + half
            value = front[k] - change[:, half * BLK : (half + 1) * BLK]
            out[pl.ds(k, PIVOTS, 8), :] = jnp.where(in_panel, 0.0, value)

    for i in range(4):

        @pl.when(group == i)
        def _():
            out[pl.ds(0, PIVOTS, 8), :] = solved[:, i * BLK : (i + 1) * BLK]

            @pl.when(leaf < 4)
            def _():
                rows = pl.ds(pl.multiple_of((leaf & 3) * BLK, BLK), BLK)
                out[pl.ds(0, BLK, 8), :] = l_ref[rows, i * BLK : (i + 1) * BLK]


def finish(place, front, columns, rows, factor, inverse):
    return pl.pallas_call(
        trailing_kernel,
        out_shape=jax.ShapeDtypeStruct((8 * PIVOTS, BLK), F32),
        in_specs=[pl.BlockSpec(memory_space=SMEM)] + [pl.BlockSpec(memory_space=VMEM)] * 11,
        out_specs=pl.BlockSpec(memory_space=VMEM),
        scratch_shapes=[VMEM((4, PIVOTS, BLK), F32), VMEM((4, 8, BLK, BLK), F32)],
        compiler_params=pltpu.CompilerParams(vmem_limit_bytes=48 * 2**20),
        cost_estimate=pl.CostEstimate(
            flops=5 * 10**9, bytes_accessed=12 * 2**20, transcendentals=0
        ),
    )(place, front, *columns, *rows, factor, inverse)


def group_swap(x, mask, sources=GROUPS):
    return lax.ppermute(x, GROUP, [(a, a ^ mask) for a in range(sources)])


def leaf_column(x, leaf):
    sent = [lax.ppermute(x, "leaf", [(y, 4 * to + y) for y in range(4)]) for to in (1, 2, 3)]
    return jnp.where(leaf < 4, x, sent[0] + sent[1] + sent[2])


def leaf_row(x):
    turned = [
        lax.ppermute(x, "leaf", [(a, (a & 12) | ((a + by) & 3)) for a in range(LEAVES)])
        for by in (1, 2, 3)
    ]
    return [x] + turned


def panel_columns(x, group):
    near = group_swap(x, 1, 4)
    far = group_swap(x, 4, 4)
    across = group_swap(x, 5, 4)
    mine = group < 4
    first = jnp.where(mine, x, far)
    second = jnp.where(mine, near, across)
    return [first, second, group_swap(first, 2), group_swap(second, 2)]


def local(pivot_block, coupling, parent_front, child_map):
    leaf = lax.axis_index("leaf")
    group = lax.axis_index(GROUP)
    place = jnp.stack([leaf, group]).astype(jnp.int32)
    coupled = coupling[0]
    others = [group_swap(coupled, mask) for mask in (1, 5, 4)]
    factor, below, inverses = factor_child(pivot_block[0], coupled)
    below_near, below_across, below_far = solve_rows(factor, inverses, others)
    have = {0: below, 1: below_near, 5: below_across, 4: below_far}
    have.update({mask ^ 2: group_swap(x, 2) for mask, x in list(have.items())})
    products = update_blocks(place, child_map, [have[s] for s in range(GROUPS)])
    got = lax.all_to_all(products, "leaf", split_axis=0, concat_axis=0, tiled=True)
    front = assemble(place, child_map, got, parent_front.reshape(8 * PIVOTS, BLK))
    diag_rows = leaf_row(leaf_column(front[0, :BLK], leaf))
    turn = [diag_rows[i] for i in range(4)]
    spot = leaf & 3
    ordered = jnp.stack(turn)[(spot - jnp.arange(4)) & 3].reshape(PIVOTS, BLK)
    panel_factor, panel_inverse = factor_panel(place, panel_columns(ordered, group))
    columns = panel_columns(front[0], group)
    rows = leaf_row(leaf_column(front[:, :BLK], leaf))
    result = finish(place, front, columns, rows, panel_factor, panel_inverse)
    factor_own = lax.dynamic_slice_in_dim(factor, group * NB, NB, 0)
    return (
        factor_own[None],
        below[None],
        result.reshape(4, 1, BLK, 8, 1, BLK),
    )


def solution(mesh):
    return jax.shard_map(
        local,
        mesh=mesh,
        in_specs=(
            P("leaf", None, None),
            P("leaf", GROUP, None),
            P(None, "leaf", None, None, GROUP, None),
            P(),
        ),
        out_specs=(
            P("leaf", GROUP, None),
            P("leaf", GROUP, None),
            P(None, "leaf", None, None, GROUP, None),
        ),
        check_vma=False,
    )
```

time: 1940 us -> 353 us (0.18)
  other arithmetic: 795 us -> 0.87 us
  waiting for transfers between devices: 678 us -> 49.6 us
  Pallas kernels: 0 us -> 236 us
  local copies, waits for them, and re-layouts: 234 us -> 5.38 us
  matrix products: 186 us -> 0 us
  starting transfers between devices: 7.71 us -> 52.8 us
  between operations: 29.5 us -> 1.46 us
    another operation x88 -> x2, other arithmetic: 751 us -> 0.61 us  [the longest x1 0.59 us: local(): place = jnp.stack([leaf, group]).astype(jnp.int32)]
    all_gather x3 -> x0, waiting for transfers between devices: 365 us -> none  [the longest x1 247 us: local(): below_all = lax.all_gather(below_own, ('row', 'col'), axis=0, tiled=True)]
    psum x4 -> x0, waiting for transfers between devices: 290 us -> none  [the longest x2 170 us: local(): diag_low, diag_high = lax.psum((diag_low, diag_high), 'leaf')]
    pallas_call x0 -> x6, Pallas kernels: none -> 236 us  [the longest x1 155 us: factor_child(): pl.pallas_call(factor_kernel, out_shape=(jax.ShapeDtypeStruct((S, S), F32...]
    another operation x86 -> x0, matrix products: 114 us -> none  [the longest x58 92.1 us: solve_right(): lax.linalg.triangular_solve(factor, rhs_rows, left_side=False, lower=True...]
    another operation x134 -> x0, local copies, waits for them, and re-layouts: 106 us -> none
    dot_general x8 -> x0, matrix products: 72.3 us -> none  [the longest x3 32.5 us: blocked_cholesky(): jnp.dot(lower_part, lower_part.T, precision=HIGHEST_PREC, preferred_eleme...]
    ppermute x0 -> x29, starting transfers between devices: none -> 45.9 us  [the longest x17 24.8 us: group_swap(): return lax.ppermute(x, GROUP, [(a, a ^ mask) for a in range(sources)])]
  transfers between devices with their start and end apart: 8 -> 30, of which waited for: 8 -> 9; matrix products, arithmetic and copies ran while one was open for 2% -> 1% of each run, Pallas kernels for 0% -> 60%
where the time goes in v1:
time: 353 us; the launch traced here: 347 us
  Pallas kernels  236 us (67%)
  starting transfers between devices  52.8 us (15%)
  waiting for transfers between devices  49.6 us (14%)
  local copies, waits for them, and re-layouts  5.38 us (2%)
    pallas_call x1, Pallas kernels, factor_child(): pl.pallas_call(factor_kernel, out_shape=(jax.ShapeDtypeStruct((S, S), F32...  155 us
    all_to_all x1, waiting for transfers between devices, local(): lax.all_to_all(products, 'leaf', split_axis=0, concat_axis=0, tiled=True)  30.7 us
    pallas_call x1, Pallas kernels, solve_rows(): pl.pallas_call(solve_kernel, out_shape=(jax.ShapeDtypeStruct((NB, S), F32...  28.6 us
    pallas_call x1, Pallas kernels, factor_panel(): pl.pallas_call(panel_kernel, out_shape=(jax.ShapeDtypeStruct((PIVOTS, PIV...  25.7 us
    ppermute x17, starting transfers between devices, group_swap(): return lax.ppermute(x, GROUP, [(a, a ^ mask) for a in range(sources)])  24.8 us
    pallas_call x1, Pallas kernels, update_blocks(): pl.pallas_call(update_kernel, out_shape=jax.ShapeDtypeStruct((LEAVES, 2,...  16.8 us
    ppermute x6, starting transfers between devices, leaf_column(): lax.ppermute(x, 'leaf', [(y, 4 * to + y) for y in range(4)])  13.2 us
    ppermute x17, waiting for transfers between devices, group_swap(): return lax.ppermute(x, GROUP, [(a, a ^ mask) for a in range(sources)])  12.6 us
  transfers between devices with their start and end apart: 30, of which 9 were waited for; matrix products, arithmetic and copies ran while one was open for 1% of the time, Pallas kernels for 60%

profile of v1, /device:TPU:0, one launch (start us, length us, event | category | flops | bytes accessed | tf_op | source)
XLA Modules:
  0.0 346.6 jit_solution(8523460035268917271)
XLA Ops:
  0.6 4.0 %collective-permute-start.2 = (f32[256,2048]{1,0:T(8,128)}, f32[256,2048]{1,0:T(8,128)}, u32[]{:S(2)}, u32[]{:S(2)}) collective-permute-start(f32[256,2048]{1,0:T(8,128)} %bitcast.36), channel_id=1, source_target_pairs={{0,4},{1,5},{2,6},{3,7},{4,0},{5,1},{6,2},{7,3},{8,12},{9,13},{10,... | collective-permute-start | bytes 6291464 | tf_op jit(solution)/shard_map/ppermute | solution.py:479
  4.7 0.7 collective-permute-start.1
  5.4 0.3 collective-permute-start
  5.7 154.8 %shard_map.67 = (f32[2048,2048]{1,0:T(8,128)}, f32[256,2048]{1,0:T(8,128)}, f32[8,256,256]{2,1,0:T(8,128)}) custom-call(bf16[2048,2048]{1,0:T(8,128)(2,1)} %bitcast.35, f32[256,2048]{1,0:T(8,128)} %bitcast.39), custom_call_target="tpu_custom_call" | custom-call | flops 149999992832 | bytes 31457280 | tf_op jit(solution)/shard_map/pallas_call | solution.py:178
  160.5 0.2 collective-permute-start.3
  160.7 28.6 %shard_map.68 = (f32[256,2048]{1,0:T(8,128)}, f32[256,2048]{1,0:T(8,128)}, f32[256,2048]{1,0:T(8,128)}) custom-call(f32[2048,2048]{1,0:T(8,128)} %get-tuple-element.11.l_hbm, f32[8,256,256]{2,1,0:T(8,128)} %get-tuple-element.13.inv_ref, f32[256,2048]{1,0:T(8,128)} %collective-permute-done.refs_0_, f32[256,2048]{1,0:T(8,128)} %collective-permute-done.1.refs_1_, ...), custom_call_target="tpu_custom_call" | custom-call | flops 20000000000 | bytes 25165824 | tf_op jit(solution)/shard_map/pallas_call | solution.py:243
  189.2 0.6 collective-permute-start.4
  189.8 0.1 collective-permute-start.5
  189.9 0.6 collective-permute-start.6
  190.5 0.6 pad_add_fusion.place
  191.1 2.8 collective-permute-done.4.refs_3_
  193.9 3.0 collective-permute-done.5.refs_6_
  196.9 3.0 collective-permute-done.6.refs_7_
  199.9 16.8 %shard_map.69 = f32[16,2,128,128]{3,2,1,0:T(8,128)} custom-call(s32[2]{0:T(128)} %pad_add_fusion.place, s32[16,16]{1,0:T(8,128)} %map_ref.3, f32[256,2048]{1,0:T(8,128)} %get-tuple-element.12.refs_0_, f32[256,2048]{1,0:T(8,128)} %get-tuple-element.14.refs_1_, f32[256,2048]{1,0:T(8,128)} %copy-done.5, f32[256,2048]{1,0:T(8,128)} %collective-permute-done.4.refs_3_, ...), custom_call_target="tpu_custom_call" | custom-call | flops 8000000000 | bytes 20971520 | tf_op jit(solution)/shard_map/pallas_call | solution.py:316
  216.7 6.9 %all-to-all-start = ((f32[16,2,128,128]{3,2,1,0:T(8,128)}), f32[16,2,128,128]{3,2,1,0:T(8,128)S(1)}, u32[]{:S(2)}, u32[]{:S(2)}) async-start(f32[16,2,128,128]{3,2,1,0:T(8,128)} %shard_map.69), calls=%async_computation | async-start | bytes 4194304 | tf_op jit(solution)/shard_map/all_to_all | solution.py:516
  223.7 30.7 %all-to-all-done.got = f32[16,2,128,128]{3,2,1,0:T(8,128)S(1)} async-done(((f32[16,2,128,128]{3,2,1,0:T(8,128)}), f32[16,2,128,128]{3,2,1,0:T(8,128)S(1)}, u32[]{:S(2)}, u32[]{:S(2)}) %all-to-all-start) | async-done | bytes 2097184 | tf_op jit(solution)/shard_map/all_to_all | solution.py:516
  254.4 1.6 copy-done.2
  255.9 2.3 shard_map.70.front
  258.3 3.4 collective-permute-start.20
  261.7 1.3 collective-permute-start.19
  263.0 1.3 collective-permute-start.18
  264.3 0.6 collective-permute-done.19
  264.9 1.3 collective-permute-done.18
  266.2 2.1 collective-permute-start.23
  268.3 0.3 collective-permute-start.22
  268.7 1.1 collective-permute-start.21
  269.8 3.8 %collective-permute-start.8 = (f32[512,128]{1,0:T(8,128)S(1)}, f32[512,128]{1,0:T(8,128)S(1)}, u32[]{:S(2)}, u32[]{:S(2)}) collective-permute-start(f32[512,128]{1,0:T(8,128)S(1)} %slice_bitcast_fusion), channel_id=1, source_target_pairs={{0,1},{1,0},{2,3},{3,2},{8,9},{9,8},{10,11},{11,10},{16,17},{17,16... | collective-permute-start | bytes 786440 | tf_op jit(solution)/shard_map/ppermute | solution.py:479
  273.7 1.5 collective-permute-start.9
  275.2 2.5 collective-permute-start.7
  277.8 0.6 gather_fusion
  278.4 2.4 collective-permute-start.24
  280.7 3.1 dynamic-slice_bitcast_fusion
  283.9 2.2 collective-permute-start.14
  286.2 3.6 %collective-permute-start.13 = (f32[8,128,128]{2,1,0:T(8,128)S(1)}, f32[8,128,128]{2,1,0:T(8,128)S(1)}, u32[]{:S(2)}, u32[]{:S(2)}) collective-permute-start(f32[8,128,128]{2,1,0:T(8,128)S(1)} %slice.15), channel_id=1, source_target_pairs={{0,64},{8,72},{16,80},{24,88},{1,65},{9,73},{17,81},{25,89},{2,66}... | collective-permute-start | bytes 1572872 | tf_op jit(solution)/shard_map/ppermute | solution.py:483
  289.9 1.3 collective-permute-start.12
  291.2 2.5 collective-permute-start.25
  293.7 4.9 %collective-permute-start.26 = (f32[512,128]{1,0:T(8,128)S(1)}, f32[512,128]{1,0:T(8,128)S(1)}, u32[]{:S(2)}, u32[]{:S(2)}) collective-permute-start(f32[512,128]{1,0:T(8,128)S(1)} %bitcast.30), channel_id=1, source_target_pairs={{0,5},{1,4},{2,7},{3,6},{8,13},{9,12},{10,15},{11,14},{16,21},{17,... | collective-permute-start | bytes 786440 | tf_op jit(solution)/shard_map/ppermute | solution.py:479
  298.7 0.8 collective-permute-done.25
  299.5 3.0 collective-permute-done.26
  302.5 0.6 collective-permute-start.28
  303.1 0.1 collective-permute-start.27
  303.2 4.5 %collective-permute-done.12 = f32[8,128,128]{2,1,0:T(8,128)S(1)} collective-permute-done((f32[8,128,128]{2,1,0:T(8,128)S(1)}, f32[8,128,128]{2,1,0:T(8,128)S(1)}, u32[]{:S(2)}, u32[]{:S(2)}) %collective-permute-start.12) | collective-permute-done | bytes 524320 | tf_op jit(solution)/shard_map/ppermute | solution.py:483
  307.7 0.1 add_select_fusion.y0
  307.8 2.3 collective-permute-start.17
  310.1 1.7 collective-permute-start.16
  311.9 0.2 collective-permute-start.15
  312.1 25.7 %shard_map.71 = (f32[512,512]{1,0:T(8,128)S(1)}, f32[512,512]{1,0:T(8,128)S(1)}) custom-call(s32[2]{0:T(128)S(1)} %copy-done.4, f32[512,128]{1,0:T(8,128)S(1)} %broadcast_select_fusion.1.d0, f32[512,128]{1,0:T(8,128)S(1)} %broadcast_select_fusion.d1, f32[512,128]{1,0:T(8,128)S(1)} %collective-permute-done.27.d2, f32[512,128]{1,0:T(8,128)S(1)} %collective-permute-done.28.d3), custom_call_target="tpu_custom_call" | custom-call | flops 24999999488 | bytes 4194304 | tf_op jit(solution)/shard_map/pallas_call | solution.py:408
  337.9 8.3 %shard_map.72 = f32[4096,128]{1,0:T(8,128)} custom-call(s32[2]{0:T(128)S(1)} %copy-done.4, f32[8,512,128]{2,1,0:T(8,128)} %copy-done, f32[512,128]{1,0:T(8,128)S(1)} %broadcast_select_fusion.3.x0, f32[512,128]{1,0:T(8,128)S(1)} %broadcast_select_fusion.2.x1, f32[512,128]{1,0:T(8,128)S(1)} %collective-permute-done.10.x2, ...), custom_call_target="tpu_custom_call" | custom-call | flops 5000000000 | bytes 12582912 | tf_op jit(solution)/shard_map/pallas_call | solution.py:465
  (45 shorter events, 0.3 us)
Async XLA Ops:
  0.6 160.0 %collective-permute-start.2 = (f32[256,2048]{1,0:T(8,128)}, f32[256,2048]{1,0:T(8,128)}, u32[]{:S(2)}, u32[]{:S(2)}) collective-permute-start(f32[256,2048]{1,0:T(8,128)} %bitcast.36), channel_id=1, source_target_pairs={{0,4},{1,5},{2,6},{3,7},{4,0},{5,1},{6,2},{7,3},{8,12},{9,13},{10,... | collective-permute-start | bytes 6291464 | tf_op jit(solution)/shard_map/ppermute | solution.py:479
  4.7 156.0 %collective-permute-start.1 = (f32[256,2048]{1,0:T(8,128)}, f32[256,2048]{1,0:T(8,128)}, u32[]{:S(2)}, u32[]{:S(2)}) collective-permute-start(f32[256,2048]{1,0:T(8,128)} %bitcast.37), channel_id=1, source_target_pairs={{0,5},{1,4},{2,7},{3,6},{4,1},{5,0},{6,3},{7,2},{8,13},{9,12},{10,... | collective-permute-start | bytes 6291464 | tf_op jit(solution)/shard_map/ppermute | solution.py:479
  5.4 155.3 %collective-permute-start = (f32[256,2048]{1,0:T(8,128)}, f32[256,2048]{1,0:T(8,128)}, u32[]{:S(2)}, u32[]{:S(2)}) collective-permute-start(f32[256,2048]{1,0:T(8,128)} %bitcast.38), channel_id=1, source_target_pairs={{0,1},{1,0},{2,3},{3,2},{4,5},{5,4},{6,7},{7,6},{8,9},{9,8},{10,11... | collective-permute-start | bytes 6291464 | tf_op jit(solution)/shard_map/ppermute | solution.py:479
  160.5 30.6 %collective-permute-start.3 = (f32[256,2048]{1,0:T(8,128)}, f32[256,2048]{1,0:T(8,128)S(1)}, u32[]{:S(2)}, u32[]{:S(2)}) collective-permute-start(f32[256,2048]{1,0:T(8,128)} %get-tuple-element.12.refs_0_), channel_id=1, source_target_pairs={{0,2},{1,3},{2,0},{3,1},{4,6},{5,7},{6,4},{7,5},{8,10},{9,11},{10,... | collective-permute-start | bytes 6291464 | tf_op jit(solution)/shard_map/ppermute | solution.py:479
  189.2 4.7 %collective-permute-start.4 = (f32[256,2048]{1,0:T(8,128)}, f32[256,2048]{1,0:T(8,128)}, u32[]{:S(2)}, u32[]{:S(2)}) collective-permute-start(f32[256,2048]{1,0:T(8,128)} %get-tuple-element.14.refs_1_), channel_id=1, source_target_pairs={{0,2},{1,3},{2,0},{3,1},{4,6},{5,7},{6,4},{7,5},{8,10},{9,11},{10,... | collective-permute-start | bytes 6291464 | tf_op jit(solution)/shard_map/ppermute | solution.py:479
  189.8 7.1 %collective-permute-start.5 = (f32[256,2048]{1,0:T(8,128)}, f32[256,2048]{1,0:T(8,128)}, u32[]{:S(2)}, u32[]{:S(2)}) collective-permute-start(f32[256,2048]{1,0:T(8,128)} %get-tuple-element.15.refs_4_), channel_id=1, source_target_pairs={{0,2},{1,3},{2,0},{3,1},{4,6},{5,7},{6,4},{7,5},{8,10},{9,11},{10,... | collective-permute-start | bytes 6291464 | tf_op jit(solution)/shard_map/ppermute | solution.py:479
  189.9 10.0 %collective-permute-start.6 = (f32[256,2048]{1,0:T(8,128)}, f32[256,2048]{1,0:T(8,128)}, u32[]{:S(2)}, u32[]{:S(2)}) collective-permute-start(f32[256,2048]{1,0:T(8,128)} %get-tuple-element.16.refs_5_), channel_id=1, source_target_pairs={{0,2},{1,3},{2,0},{3,1},{4,6},{5,7},{6,4},{7,5},{8,10},{9,11},{10,... | collective-permute-start | bytes 6291464 | tf_op jit(solution)/shard_map/ppermute | solution.py:479
  191.1 8.8 %copy-start.5 = (f32[256,2048]{1,0:T(8,128)}, f32[256,2048]{1,0:T(8,128)S(1)}, u32[]{:S(2)}) copy-start(f32[256,2048]{1,0:T(8,128)S(1)} %collective-permute-done.3.refs_2_) | copy-start | bytes 6291460
  216.7 37.6 %copy-start.3 = (s32[16,16]{1,0:T(8,128)S(1)}, s32[16,16]{1,0:T(8,128)}, u32[]{:S(2)}) copy-start(s32[16,16]{1,0:T(8,128)} %map_ref.3) | copy-start | bytes 3076
  216.7 37.6 %copy-start.4 = (s32[2]{0:T(128)S(1)}, s32[2]{0:T(128)}, u32[]{:S(2)}) copy-start(s32[2]{0:T(128)} %pad_add_fusion.place) | copy-start | bytes 28
  216.7 37.6 %all-to-all-start = ((f32[16,2,128,128]{3,2,1,0:T(8,128)}), f32[16,2,128,128]{3,2,1,0:T(8,128)S(1)}, u32[]{:S(2)}, u32[]{:S(2)}) async-start(f32[16,2,128,128]{3,2,1,0:T(8,128)} %shard_map.69), calls=%async_computation | async-start | bytes 4194304 | tf_op jit(solution)/shard_map/all_to_all | solution.py:516
  254.3 1.6 copy-start.2
  258.3 11.5 %copy-start = (f32[8,512,128]{2,1,0:T(8,128)}, f32[8,512,128]{2,1,0:T(8,128)S(1)}, u32[]{:S(2)}) copy-start(f32[8,512,128]{2,1,0:T(8,128)S(1)} %shard_map.70.front) | copy-start | bytes 6291460
  258.3 6.0 %collective-permute-start.20 = (f32[128,128]{1,0:T(8,128)S(1)}, f32[128,128]{1,0:T(8,128)S(1)}, u32[]{:S(2)}, u32[]{:S(2)}) collective-permute-start(f32[128,128]{1,0:T(8,128)S(1)} %slice_bitcast_fusion.1), channel_id=1, source_target_pairs={{0,96},{8,104},{16,112},{24,120},{1,97},{9,105},{17,113},{25,121},... | collective-permute-start | bytes 196616 | tf_op jit(solution)/shard_map/ppermute | solution.py:483
  261.7 3.2 collective-permute-start.19
  263.0 3.2 collective-permute-start.18
  266.2 9.0 %collective-permute-start.23 = (f32[128,128]{1,0:T(8,128)S(1)}, f32[128,128]{1,0:T(8,128)S(1)}, u32[]{:S(2)}, u32[]{:S(2)}) collective-permute-start(f32[128,128]{1,0:T(8,128)S(1)} %add_select_fusion.1), channel_id=1, source_target_pairs={{0,24},{8,0},{16,8},{24,16},{32,56},{40,32},{48,40},{56,48},{64,88... | collective-permute-start | bytes 196616 | tf_op jit(solution)/shard_map/ppermute | solution.py:489
  268.3 9.4 %collective-permute-start.22 = (f32[128,128]{1,0:T(8,128)S(1)}, f32[128,128]{1,0:T(8,128)S(1)}, u32[]{:S(2)}, u32[]{:S(2)}) collective-permute-start(f32[128,128]{1,0:T(8,128)S(1)} %add_select_fusion.1), channel_id=1, source_target_pairs={{0,16},{8,24},{16,0},{24,8},{32,48},{40,56},{48,32},{56,40},{64,80... | collective-permute-start | bytes 196616 | tf_op jit(solution)/shard_map/ppermute | solution.py:489
  268.7 9.1 %collective-permute-start.21 = (f32[128,128]{1,0:T(8,128)S(1)}, f32[128,128]{1,0:T(8,128)S(1)}, u32[]{:S(2)}, u32[]{:S(2)}) collective-permute-start(f32[128,128]{1,0:T(8,128)S(1)} %add_select_fusion.1), channel_id=1, source_target_pairs={{0,8},{8,16},{16,24},{24,0},{32,40},{40,48},{48,56},{56,32},{64,72... | collective-permute-start | bytes 196616 | tf_op jit(solution)/shard_map/ppermute | solution.py:489
  269.8 20.0 %collective-permute-start.8 = (f32[512,128]{1,0:T(8,128)S(1)}, f32[512,128]{1,0:T(8,128)S(1)}, u32[]{:S(2)}, u32[]{:S(2)}) collective-permute-start(f32[512,128]{1,0:T(8,128)S(1)} %slice_bitcast_fusion), channel_id=1, source_target_pairs={{0,1},{1,0},{2,3},{3,2},{8,9},{9,8},{10,11},{11,10},{16,17},{17,16... | collective-permute-start | bytes 786440 | tf_op jit(solution)/shard_map/ppermute | solution.py:479
  273.7 17.5 %collective-permute-start.9 = (f32[512,128]{1,0:T(8,128)S(1)}, f32[512,128]{1,0:T(8,128)S(1)}, u32[]{:S(2)}, u32[]{:S(2)}) collective-permute-start(f32[512,128]{1,0:T(8,128)S(1)} %slice_bitcast_fusion), channel_id=1, source_target_pairs={{0,5},{1,4},{2,7},{3,6},{8,13},{9,12},{10,15},{11,14},{16,21},{17,... | collective-permute-start | bytes 786440 | tf_op jit(solution)/shard_map/ppermute | solution.py:479
  275.2 10.9 %collective-permute-start.7 = (f32[512,128]{1,0:T(8,128)S(1)}, f32[512,128]{1,0:T(8,128)}, u32[]{:S(2)}, u32[]{:S(2)}) collective-permute-start(f32[512,128]{1,0:T(8,128)S(1)} %slice_bitcast_fusion), channel_id=1, source_target_pairs={{0,4},{1,5},{2,6},{3,7},{8,12},{9,13},{10,14},{11,15},{16,20},{17,... | collective-permute-start | bytes 786440 | tf_op jit(solution)/shard_map/ppermute | solution.py:479
  278.4 5.5 %copy-start.1 = (f32[8,512,128]{2,1,0:T(8,128)S(1)}, f32[8,512,128]{2,1,0:T(8,128)}, u32[]{:S(2)}) copy-start(f32[8,512,128]{2,1,0:T(8,128)} %copy-done) | copy-start | bytes 6291460
  278.4 15.3 %collective-permute-start.24 = (f32[512,128]{1,0:T(8,128)S(1)}, f32[512,128]{1,0:T(8,128)S(1)}, u32[]{:S(2)}, u32[]{:S(2)}) collective-permute-start(f32[512,128]{1,0:T(8,128)S(1)} %bitcast.28), channel_id=1, source_target_pairs={{0,4},{1,5},{2,6},{3,7},{8,12},{9,13},{10,14},{11,15},{16,20},{17,... | collective-permute-start | bytes 786440 | tf_op jit(solution)/shard_map/ppermute | solution.py:479
  283.9 18.6 %collective-permute-start.14 = (f32[8,128,128]{2,1,0:T(8,128)S(1)}, f32[8,128,128]{2,1,0:T(8,128)S(1)}, u32[]{:S(2)}, u32[]{:S(2)}) collective-permute-start(f32[8,128,128]{2,1,0:T(8,128)S(1)} %slice.15), channel_id=1, source_target_pairs={{0,96},{8,104},{16,112},{24,120},{1,97},{9,105},{17,113},{25,121},... | collective-permute-start | bytes 1572872 | tf_op jit(solution)/shard_map/ppermute | solution.py:483
  286.2 17.0 %collective-permute-start.13 = (f32[8,128,128]{2,1,0:T(8,128)S(1)}, f32[8,128,128]{2,1,0:T(8,128)S(1)}, u32[]{:S(2)}, u32[]{:S(2)}) collective-permute-start(f32[8,128,128]{2,1,0:T(8,128)S(1)} %slice.15), channel_id=1, source_target_pairs={{0,64},{8,72},{16,80},{24,88},{1,65},{9,73},{17,81},{25,89},{2,66}... | collective-permute-start | bytes 1572872 | tf_op jit(solution)/shard_map/ppermute | solution.py:483
  289.9 17.8 %collective-permute-start.12 = (f32[8,128,128]{2,1,0:T(8,128)S(1)}, f32[8,128,128]{2,1,0:T(8,128)S(1)}, u32[]{:S(2)}, u32[]{:S(2)}) collective-permute-start(f32[8,128,128]{2,1,0:T(8,128)S(1)} %slice.15), channel_id=1, source_target_pairs={{0,32},{8,40},{16,48},{24,56},{1,33},{9,41},{17,49},{25,57},{2,34}... | collective-permute-start | bytes 1572872 | tf_op jit(solution)/shard_map/ppermute | solution.py:483
  291.2 8.3 %collective-permute-start.25 = (f32[512,128]{1,0:T(8,128)S(1)}, f32[512,128]{1,0:T(8,128)S(1)}, u32[]{:S(2)}, u32[]{:S(2)}) collective-permute-start(f32[512,128]{1,0:T(8,128)S(1)} %bitcast.29), channel_id=1, source_target_pairs={{0,1},{1,0},{2,3},{3,2},{8,9},{9,8},{10,11},{11,10},{16,17},{17,16... | collective-permute-start | bytes 786440 | tf_op jit(solution)/shard_map/ppermute | solution.py:479
  293.7 8.8 %collective-permute-start.26 = (f32[512,128]{1,0:T(8,128)S(1)}, f32[512,128]{1,0:T(8,128)S(1)}, u32[]{:S(2)}, u32[]{:S(2)}) collective-permute-start(f32[512,128]{1,0:T(8,128)S(1)} %bitcast.30), channel_id=1, source_target_pairs={{0,5},{1,4},{2,7},{3,6},{8,13},{9,12},{10,15},{11,14},{16,21},{17,... | collective-permute-start | bytes 786440 | tf_op jit(solution)/shard_map/ppermute | solution.py:479
  299.5 38.4 %collective-permute-start.11 = (f32[512,128]{1,0:T(8,128)S(1)}, f32[512,128]{1,0:T(8,128)S(1)}, u32[]{:S(2)}, u32[]{:S(2)}) collective-permute-start(f32[512,128]{1,0:T(8,128)S(1)} %broadcast_select_fusion.2.x1), channel_id=1, source_target_pairs={{0,2},{1,3},{2,0},{3,1},{4,6},{5,7},{6,4},{7,5},{8,10},{9,11},{10,... | collective-permute-start | bytes 786440 | tf_op jit(solution)/shard_map/ppermute | solution.py:479
  302.5 35.3 %collective-permute-start.10 = (f32[512,128]{1,0:T(8,128)S(1)}, f32[512,128]{1,0:T(8,128)S(1)}, u32[]{:S(2)}, u32[]{:S(2)}) collective-permute-start(f32[512,128]{1,0:T(8,128)S(1)} %broadcast_select_fusion.3.x0), channel_id=1, source_target_pairs={{0,2},{1,3},{2,0},{3,1},{4,6},{5,7},{6,4},{7,5},{8,10},{9,11},{10,... | collective-permute-start | bytes 786440 | tf_op jit(solution)/shard_map/ppermute | solution.py:479
  302.5 7.6 %collective-permute-start.28 = (f32[512,128]{1,0:T(8,128)S(1)}, f32[512,128]{1,0:T(8,128)S(1)}, u32[]{:S(2)}, u32[]{:S(2)}) collective-permute-start(f32[512,128]{1,0:T(8,128)S(1)} %broadcast_select_fusion.d1), channel_id=1, source_target_pairs={{0,2},{1,3},{2,0},{3,1},{4,6},{5,7},{6,4},{7,5},{8,10},{9,11},{10,... | collective-permute-start | bytes 786440 | tf_op jit(solution)/shard_map/ppermute | solution.py:479
  303.1 8.7 %collective-permute-start.27 = (f32[512,128]{1,0:T(8,128)S(1)}, f32[512,128]{1,0:T(8,128)S(1)}, u32[]{:S(2)}, u32[]{:S(2)}) collective-permute-start(f32[512,128]{1,0:T(8,128)S(1)} %broadcast_select_fusion.1.d0), channel_id=1, source_target_pairs={{0,2},{1,3},{2,0},{3,1},{4,6},{5,7},{6,4},{7,5},{8,10},{9,11},{10,... | collective-permute-start | bytes 786440 | tf_op jit(solution)/shard_map/ppermute | solution.py:479
  307.8 30.1 %collective-permute-start.17 = (f32[8,128,128]{2,1,0:T(8,128)S(1)}, f32[8,128,128]{2,1,0:T(8,128)S(1)}, u32[]{:S(2)}, u32[]{:S(2)}) collective-permute-start(f32[8,128,128]{2,1,0:T(8,128)S(1)} %add_select_fusion.y0), channel_id=1, source_target_pairs={{0,24},{8,0},{16,8},{24,16},{32,56},{40,32},{48,40},{56,48},{64,88... | collective-permute-start | bytes 1572872 | tf_op jit(solution)/shard_map/ppermute | solution.py:489
  310.1 27.7 %collective-permute-start.16 = (f32[8,128,128]{2,1,0:T(8,128)S(1)}, f32[8,128,128]{2,1,0:T(8,128)S(1)}, u32[]{:S(2)}, u32[]{:S(2)}) collective-permute-start(f32[8,128,128]{2,1,0:T(8,128)S(1)} %add_select_fusion.y0), channel_id=1, source_target_pairs={{0,16},{8,24},{16,0},{24,8},{32,48},{40,56},{48,32},{56,40},{64,80... | collective-permute-start | bytes 1572872 | tf_op jit(solution)/shard_map/ppermute | solution.py:489
  311.9 26.0 %collective-permute-start.15 = (f32[8,128,128]{2,1,0:T(8,128)S(1)}, f32[8,128,128]{2,1,0:T(8,128)S(1)}, u32[]{:S(2)}, u32[]{:S(2)}) collective-permute-start(f32[8,128,128]{2,1,0:T(8,128)S(1)} %add_select_fusion.y0), channel_id=1, source_target_pairs={{0,8},{8,16},{16,24},{24,0},{32,40},{40,48},{48,56},{56,32},{64,72... | collective-permute-start | bytes 1572872 | tf_op jit(solution)/shard_map/ppermute | solution.py:489
